TPU v7x, 128 devices: a whole 4x4x4 slice. The times are simulated.
128 devices in a mesh: dp: 16 (over z, y_lo, core), mp: 8 (over y_hi, x).
Axes of the slice: x: 4, y: 4 (y_hi: 2, y_lo: 2; y = y_hi * 2 + y_lo), z: 4, core: 2. Of those that a mesh axis runs over, the one named last changes fastest.
Arguments:
- out_grad: bfloat16 [16384, 4096], P(('dp', 'mp')), may hold values from -24 to 24
- gate_pre: bfloat16 [16384, 14336], P('dp', 'mp'), may hold values from -6 to 6
- up_pre: bfloat16 [16384, 14336], P('dp', 'mp'), may hold values from -6 to 6
- down_weight: bfloat16 [14336, 4096], P('mp', 'dp'), may hold values from -0.046875 to 0.046875
Outputs:
- grad_gate_pre: bfloat16 [16384, 14336], P('dp', 'mp')
- grad_up_pre: bfloat16 [16384, 14336], P('dp', 'mp')
- grad_down: bfloat16 [14336, 4096], P('mp', 'dp')
All inputs are finite; a program needn't handle non-finite values.
Results may differ from a plain program's by a relative error of at most 0.022.
Values may be sent and summed in bfloat16 or wider, within the bound.
A program may use at most 128 MiB of HBM per device.

v0:
```python
import math

import jax
import jax.numpy as jnp
from jax import lax
from jax.sharding import PartitionSpec as P


def shards(out_grad, gate_pre, up_pre, down_weight):
    token_count = out_grad.shape[0] * lax.axis_size("mp") * lax.axis_size("dp")
    norm_scale = 1.0 / math.sqrt(token_count)
    full_rows = lax.all_gather(out_grad, "mp", axis=0, tiled=True)
    gate_float = gate_pre.astype(jnp.float32)
    up_float = up_pre.astype(jnp.float32)
    sigmoid_gate = jax.nn.sigmoid(gate_float)
    silu_gate = gate_float * sigmoid_gate
    hidden = (silu_gate * up_float).astype(jnp.bfloat16)
    d_hidden = lax.dot_general(
        full_rows,
        lax.all_gather(down_weight, "dp", axis=1, tiled=True),
        (((1,), (1,)), ((), ())),
        preferred_element_type=jnp.float32,
    )
    term = lax.dot_general(
        full_rows, hidden, (((0,), (0,)), ((), ())), preferred_element_type=jnp.float32
    )
    summed = lax.psum_scatter(
        lax.optimization_barrier(term.astype(jnp.bfloat16))
        .astype(jnp.float32)
        .astype(jnp.bfloat16),
        "dp",
        scatter_dimension=0,
        tiled=True,
    ).astype(jnp.float32)
    grad_down = (summed * norm_scale).astype(jnp.bfloat16).T
    grad_gate = (
        d_hidden * up_float * sigmoid_gate * (1.0 + gate_float * (1.0 - sigmoid_gate))
    ).astype(jnp.bfloat16)
    grad_up = (d_hidden * silu_gate).astype(jnp.bfloat16)
    return (grad_gate, grad_up, grad_down)


def solution(mesh):
    return jax.shard_map(
        shards,
        mesh=mesh,
        in_specs=(P(("dp", "mp"), None), P("dp", "mp"), P("dp", "mp"), P("mp", "dp")),
        out_specs=(P("dp", "mp"), P("dp", "mp"), P("mp", "dp")),
        check_vma=False,
    )
```

profile of v0, /device:TPU:0, one launch (start us, length us, event | category | flops | bytes accessed | tf_op | source)
XLA Modules:
  0.0 383.3 jit_solution(6733214664956503063)
XLA Ops:
  7.2 0.0 all-gather.3.cloned.1.call-start
  7.2 0.7 all-gather.3.cloned.1.call-update
  7.9 0.0 all-gather.5.cloned.1.call-start
  7.9 0.7 all-gather.5.cloned.1.call-update
  8.6 0.0 reduce-scatter.2.cloned.1.call-start
  8.7 113.0 %all-gather.3.cloned.1.call-done = bf16[1024,4096]{1,0:T(8,128)(2,1)} async-done(((bf16[128,4096]{1,0:T(8,128)(2,1)}), bf16[1024,4096]{1,0:T(8,128)(2,1)}) %all-gather.3.cloned.1.call-update) | async-done | bytes 8388624 | tf_op jit(solution)/shard_map/all_gather | solution.py:12
  121.7 23.7 %fusion = bf16[4096,1792]{0,1:T(8,128)(2,1)} fusion(bf16[1024,4096]{1,0:T(8,128)(2,1)} %all-gather.3.cloned.1.call-done, bf16[1024,1792]{1,0:T(8,128)(2,1)} %param.6, bf16[1024,1792]{1,0:T(8,128)(2,1)} %param.5), kind=kOutput, calls=%fused_computation.1 | convolution fusion | flops 15054405632 | bytes 30408704 | tf_op jit(solution)/shard_map/dot_general | solution.py:24
  145.4 0.0 reduce-scatter.2.cloned.1.call-update
  145.4 65.3 %all-gather.5.cloned.1.call-done = bf16[1792,4096]{1,0:T(8,128)(2,1)} async-done(((bf16[1792,256]{1,0:T(8,128)(2,1)}), bf16[1792,4096]{1,0:T(8,128)(2,1)}) %all-gather.5.cloned.1.call-update) | async-done | bytes 14680080 | tf_op jit(solution)/shard_map/all_gather | solution.py:20
  210.7 26.4 %multiply_convert_fusion = (bf16[1024,1792]{1,0:T(8,128)(2,1)}, bf16[1024,1792]{1,0:T(8,128)(2,1)}) fusion(bf16[1024,1792]{1,0:T(8,128)(2,1)} %param.5, bf16[1024,1792]{1,0:T(8,128)(2,1)} %param.6, bf16[1024,4096]{1,0:T(8,128)(2,1)} %all-gather.3.cloned.1.call-done, bf16[1792,4096]{1,0:T(8,128)(2,1)} %all-gather.5.cloned.1.call-done), kind=kOutput, calls=%fused_computation.15 | convolution fusion | flops 15059910656 | bytes 37748736 | tf_op jit(solution)/shard_map/dot_general | solution.py:18
  237.2 137.3 %reduce-scatter.2.cloned.1.call-done = bf16[256,1792]{0,1:T(8,128)(2,1)} async-done(((bf16[4096,1792]{0,1:T(8,128)(2,1)}), bf16[256,1792]{0,1:T(8,128)(2,1)}) %reduce-scatter.2.cloned.1.call-update) | async-done | bytes 917520 | tf_op jit(solution)/shard_map/reduce_scatter | solution.py:27
  374.5 2.3 fusion.10
Async XLA Ops:
  7.2 114.5 %all-gather.3.cloned.1.call-start = ((), (), s32[]{:S(2)}) async-start(), calls=%async_computation.1 | async-start | bytes 9437184 | tf_op jit(solution)/shard_map/all_gather | solution.py:12
  7.9 202.8 %all-gather.5.cloned.1.call-start = ((), (), s32[]{:S(2)}) async-start(), calls=%async_computation.2 | async-start | bytes 15597568 | tf_op jit(solution)/shard_map/all_gather | solution.py:20
  8.6 365.8 %reduce-scatter.2.cloned.1.call-start = ((), (), s32[]{:S(2)}) async-start(), calls=%async_computation.3 | async-start | bytes 15597568 | tf_op jit(solution)/shard_map/reduce_scatter | solution.py:27
Sparse Core Ops, SparseCore 0:
  10.3 111.3 all-gather.2
  123.3 87.3 all-gather.4
  213.2 161.2 reduce-scatter.1
where the time goes:
time: 383 us
  waiting for transfers between devices  317 us (83%)
  matrix products  50.1 us (13%)
  between operations  13.7 us (4%)
    reduce_scatter x1, waiting for transfers between devices, shards(): lax.psum_scatter(lax.optimization_barrier(term.astype(jnp.bfloat16)).asty...  137 us
    all_gather x1, waiting for transfers between devices, shards(): full_rows = lax.all_gather(out_grad, 'mp', axis=0, tiled=True)  113 us
    all_gather x1, waiting for transfers between devices, shards(): lax.all_gather(down_weight, 'dp', axis=1, tiled=True)  65.3 us
    dot_general x1, matrix products, shards(): lax.dot_general(full_rows, lax.all_gather(down_weight, 'dp', axis=1, tile...  26.4 us
    dot_general x1, matrix products, shards(): lax.dot_general(full_rows, hidden, (((0,), (0,)), ((), ())), preferred_el...  23.7 us
  transfers between devices with their start and end apart: 3, of which 3 were waited for; matrix products, arithmetic and copies ran while one was open for 13% of the time, Pallas kernels for 0%

commit v1 on v0

v1 whole, which is shorter than its diff:
```python
import math

import jax
import jax.numpy as jnp
from jax import lax
from jax.experimental import pallas as pl
from jax.experimental.pallas import tpu as pltpu
from jax.sharding import PartitionSpec as P

MESH = pl.DeviceIdType.MESH
F32 = jnp.float32
BF16 = jnp.bfloat16

ORDER = ((2, 1), (2, 0), (1, 1), (-1, 1), (1, 0), (-1, 0), (0, 1), (0, 0))
SLOT = {at: k for k, at in enumerate(ORDER)}
LAG = 2


def kernel(
    og, gp, up, w, gg, gu, gd,
    o_all, w_all, h_t, own, pre, snd, half_in, full_in, y_in, acc, gbuf, ubuf, ggbuf, gubuf,
    o_send, o_recv, w_send, w_recv, wc_send, wc_recv, t_send, t_recv, z_send, z_recv, y_send, y_recv,
    o_local, w_local, in_sem, out_sem, gd_sem,
):
    TB = og.shape[0]
    BLK = w.shape[1]
    FFD = w.shape[0]
    TOK = gp.shape[0]
    HALF = FFD // 2
    TH = TB // 2
    NT = FFD // BLK
    norm = 1.0 / math.sqrt(TOK * 16)

    dp = lax.axis_index("dp")
    mp = lax.axis_index("mp")
    z, yl, c = dp // 4, (dp // 2) % 2, dp % 2
    yh, x = mp // 4, mp % 4

    def dev(dz=0, o=0, cc=0, h=0, dx=0):
        a = ((z + dz + 4) % 4) * 4 + ((yl + o) % 2) * 2 + (c + cc) % 2
        b = ((yh + h) % 2) * 4 + (x + dx + 4) % 4
        return (a, b)

    ZP, ZM, YP, CP = dev(dz=1), dev(dz=-1), dev(o=1), dev(cc=1)
    HP, XP, XM = dev(h=1), dev(dx=1), dev(dx=-1)

    sends = []

    def send(src, dst, ss, rs, to):
        cp = pltpu.make_async_remote_copy(src, dst, ss, rs, device_id=to, device_id_type=MESH)
        cp.start()
        sends.append(cp)
        return cp

    def arrived(dst, ss, rs):
        pltpu.make_async_remote_copy(dst, dst, ss, rs, device_id=CP, device_id_type=MESH).wait_recv()

    barrier = pltpu.get_barrier_semaphore()
    for to in (ZP, ZM, YP, CP, HP, XP, XM):
        pl.semaphore_signal(barrier, inc=1, device_id=to, device_id_type=MESH)

    def tile_in(n, slot):
        cols = pl.ds(pl.multiple_of(n * BLK, BLK), BLK)
        return (
            pltpu.make_async_copy(gp.at[:, cols], gbuf.at[slot], in_sem.at[slot, 0]),
            pltpu.make_async_copy(up.at[:, cols], ubuf.at[slot], in_sem.at[slot, 1]),
        )

    def tile_out(n, slot):
        cols = pl.ds(pl.multiple_of(n * BLK, BLK), BLK)
        return (
            pltpu.make_async_copy(ggbuf.at[slot], gg.at[:, cols], out_sem.at[slot, 0]),
            pltpu.make_async_copy(gubuf.at[slot], gu.at[:, cols], out_sem.at[slot, 1]),
        )

    def o_cols(k):
        return pl.ds(k * 2 * BLK, 2 * BLK)

    def o_rows(h, dx, part=None):
        base = (((yh + h) % 2) * 4 + (x + dx + 4) % 4) * TB
        if part is None:
            return pl.ds(pl.multiple_of(base, TB), TB)
        return pl.ds(pl.multiple_of(base + part * TH, TH), TH)

    def w_cols(k, cc):
        return pl.ds((2 * k + cc) * BLK, BLK)

    w_own = pltpu.make_async_copy(w, w_all.at[:, w_cols(SLOT[0, 0], 0)], w_local)
    w_own.start()
    o_own = []
    for k, (dz, o) in enumerate(ORDER):
        for cc in range(2):
            d = ((z + dz + 4) % 4) * 4 + ((yl + o) % 2) * 2 + (c + cc) % 2
            cp = pltpu.make_async_copy(
                og.at[:, pl.ds(pl.multiple_of(d * BLK, BLK), BLK)],
                o_all.at[o_rows(0, 0), pl.ds((2 * k + cc) * BLK, BLK)],
                o_local.at[k, cc],
            )
            cp.start()
            o_own.append(cp)
    for slot in range(2):
        for cp in tile_in(slot, slot):
            cp.start()

    pl.semaphore_wait(barrier, 7)

    def w_part(k, cc, part):
        return w_all.at[pl.ds(part * HALF, HALF), w_cols(k, cc)]

    def w_to(src, k, part, sem, to):
        send(src, w_part(k, 0, part), w_send.at[sem], w_recv.at[k, part], to)

    def w_got(k, part):
        arrived(w_part(k, 0, part), w_send.at[0], w_recv.at[k, part])

    def w_share(k):
        send(
            w_all.at[:, w_cols(k, 0)], w_all.at[:, w_cols(k, 1)], wc_send.at[k], wc_recv.at[k], CP
        )

    def W0():
        a, b = w.at[pl.ds(0, HALF), :], w.at[pl.ds(HALF, HALF), :]
        w_to(a, SLOT[-1, 0], 0, 0, ZP)
        w_to(b, SLOT[1, 0], 1, 1, ZM)
        w_to(a, SLOT[0, 1], 0, 2, YP)
        w_to(b, SLOT[-1, 0], 1, 3, ZP)
        w_to(a, SLOT[1, 0], 0, 4, ZM)
        w_to(b, SLOT[0, 1], 1, 5, YP)

    def W1(o):
        w_got(SLOT[-1, o], 0)
        w_to(w_part(SLOT[-1, o], 0, 0), SLOT[2, o], 0, 6 + 2 * o, ZP)
        w_got(SLOT[1, o], 1)
        w_to(w_part(SLOT[1, o], 0, 1), SLOT[2, o], 1, 7 + 2 * o, ZM)

    def W2():
        k = SLOT[0, 1]
        w_got(k, 0)
        w_to(w_part(k, 0, 0), SLOT[-1, 1], 0, 10, ZP)
        w_to(w_part(k, 0, 0), SLOT[1, 1], 0, 11, ZM)
        w_got(k, 1)
        w_to(w_part(k, 0, 1), SLOT[1, 1], 1, 12, ZM)
        w_to(w_part(k, 0, 1), SLOT[-1, 1], 1, 13, ZP)
        w_share(k)

    def W4(o):
        w_got(SLOT[-1, o], 1)
        w_share(SLOT[-1, o])
        w_got(SLOT[1, o], 0)
        w_share(SLOT[1, o])

    def W5(o):
        k = SLOT[2, o]
        w_got(k, 0)
        w_got(k, 1)
        w_share(k)

    def o_to(k, h, dx, part, kind, to):
        ref = o_all.at[o_rows(h, dx, part), o_cols(k)]
        send(ref, ref, o_send.at[k, kind], o_recv.at[k, kind], to)

    def o_got(k, h, dx, part, kind):
        ref = o_all.at[o_rows(h, dx, part), o_cols(k)]
        arrived(ref, o_send.at[k, kind], o_recv.at[k, kind])

    def O0(k):
        o_own[2 * k].wait()
        o_own[2 * k + 1].wait()
        o_to(k, 0, 0, None, 0, HP)
        o_to(k, 0, 0, None, 1, XP)
        o_to(k, 0, 0, None, 2, XM)

    def O1(k):
        o_got(k, 0, -1, None, 1)
        o_to(k, 0, -1, 0, 3, XP)
        o_got(k, 0, 1, None, 2)
        o_to(k, 0, 1, 1, 4, XM)
        o_got(k, 1, 0, None, 0)
        o_to(k, 1, 0, None, 5, XP)
        o_to(k, 1, 0, None, 6, XM)

    def O2(k):
        o_got(k, 1, -1, None, 5)
        o_to(k, 1, -1, 0, 7, XP)
        o_got(k, 1, 1, None, 6)
        o_to(k, 1, 1, 1, 8, XM)

    def O3(k):
        o_got(k, 0, 2, 0, 3)
        o_got(k, 0, 2, 1, 4)
        o_got(k, 1, 2, 0, 7)
        o_got(k, 1, 2, 1, 8)

    def hidden_tile(n, _):
        slot = n % 2
        for cp in tile_in(n, slot):
            cp.wait()

        def rows(i, _):
            r = pl.ds(pl.multiple_of(i * 128, 128), 128)
            g = gbuf[slot, r, :].astype(F32)
            u = ubuf[slot, r, :].astype(F32)
            hid = g * jax.nn.sigmoid(g) * u
            h_t[pl.ds(pl.multiple_of(n * BLK, BLK), BLK), r] = hid.T.astype(BF16)
            return 0

        lax.fori_loop(0, TOK // 128, rows, 0)

        @pl.when(n + 2 < NT)
        def _():
            for cp in tile_in(n + 2, slot):
                cp.start()

        return 0

    def term(k, cc, dst):
        def rows(i, _):
            r = pl.ds(pl.multiple_of(i * HALF, HALF), HALF)
            dst[r, :] = jnp.dot(
                h_t[r, :], o_all[:, pl.ds((2 * k + cc) * BLK, BLK)], preferred_element_type=F32
            ).astype(BF16)
            return 0

        lax.fori_loop(0, 2, rows, 0)

    t_copies = {}

    def T(k):
        slot = k % 2
        if k >= 2:
            t_copies[k - 2].wait_send()
            sends[:] = [cp for cp in sends if cp is not t_copies[k - 2]]
        term(k, 1, snd.at[slot])
        t_copies[k] = send(snd.at[slot], pre.at[k], t_send.at[k], t_recv.at[k], CP)
        term(k, 0, own.at[k])

    def add(dst, others, start=0, size=None, scale=None):
        step = 128

        def rows(i, _):
            r = pl.ds(pl.multiple_of(start + i * step, step), step)
            total = dst[r, :].astype(F32)
            for ref, at in others:
                total += ref[pl.ds(pl.multiple_of(start - at + i * step, step), step), :].astype(F32)
            if scale is not None:
                total *= scale
            dst[r, :] = total.astype(BF16)
            return 0

        lax.fori_loop(0, size // step, rows, 0)

    def Pk(k):
        dz, o = ORDER[k]
        blk = own.at[k]
        arrived(pre.at[k], t_send.at[k], t_recv.at[k])
        up_half, down_half = pl.ds(0, HALF), pl.ds(HALF, HALF)
        if dz == 2:
            add(blk, [(pre.at[k], 0)], 0, FFD)
            send(blk.at[up_half, :], half_in.at[o, 0], z_send.at[o, 0], z_recv.at[o, 0], ZP)
            send(blk.at[down_half, :], half_in.at[o, 1], z_send.at[o, 1], z_recv.at[o, 1], ZM)
        elif dz == 1:
            add(blk, [(pre.at[k], 0)], HALF, HALF)
            arrived(half_in.at[o, 0], z_send.at[o, 0], z_recv.at[o, 0])
            add(blk, [(pre.at[k], 0), (half_in.at[o, 0], 0)], 0, HALF)
            send(blk, full_in.at[o, 0], z_send.at[o, 2], z_recv.at[o, 2], ZP)
        elif dz == -1:
            add(blk, [(pre.at[k], 0)], 0, HALF)
            arrived(half_in.at[o, 1], z_send.at[o, 1], z_recv.at[o, 1])
            add(blk, [(pre.at[k], 0), (half_in.at[o, 1], HALF)], HALF, HALF)
            send(blk, full_in.at[o, 1], z_send.at[o, 3], z_recv.at[o, 3], ZM)
        else:
            arrived(full_in.at[o, 0], z_send.at[o, 2], z_recv.at[o, 2])
            arrived(full_in.at[o, 1], z_send.at[o, 3], z_recv.at[o, 3])
            parts = [(pre.at[k], 0), (full_in.at[o, 0], 0), (full_in.at[o, 1], 0)]
            if o == 1:
                add(blk, parts, 0, FFD)
                send(blk, y_in, y_send, y_recv, YP)
            else:
                arrived(y_in, y_send, y_recv)
                add(blk, parts + [(y_in, 0)], 0, FFD, norm)
                cp = pltpu.make_async_copy(blk, gd, gd_sem)
                cp.start()
                cp.wait()

    def D(n, _):
        slot = n % 2

        def mm(i, _):
            r = pl.ds(pl.multiple_of(i * 512, 512), 512)
            acc[r, :] = lax.dot_general(
                o_all[r, :],
                w_all[pl.ds(pl.multiple_of(n * BLK, BLK), BLK), :],
                (((1,), (1,)), ((), ())),
                preferred_element_type=F32,
            )
            return 0

        lax.fori_loop(0, TOK // 512, mm, 0)
        for cp in tile_in(n, slot):
            cp.wait()

        @pl.when(n >= 2)
        def _():
            for cp in tile_out(n - 2, slot):
                cp.wait()

        def rows(i, _):
            r = pl.ds(pl.multiple_of(i * 64, 64), 64)
            g = gbuf[slot, r, :].astype(F32)
            u = ubuf[slot, r, :].astype(F32)
            d = acc[r, :]
            s = jax.nn.sigmoid(g)
            ggbuf[slot, r, :] = (d * u * s * (1.0 + g * (1.0 - s))).astype(BF16)
            gubuf[slot, r, :] = (d * (g * s)).astype(BF16)
            return 0

        lax.fori_loop(0, TOK // 64, rows, 0)
        for cp in tile_out(n, slot):
            cp.start()

        @pl.when(n + 2 < NT)
        def _():
            for cp in tile_in(n + 2, slot):
                cp.start()

        return 0

    W0()
    O0(0)
    O0(1)
    O0(2)
    lax.fori_loop(0, NT, hidden_tile, 0)
    for slot in range(2):
        for cp in tile_in(slot, slot):
            cp.start()
    w_own.wait()
    w_share(SLOT[0, 0])
    O1(0)
    W1(0)
    O1(1)
    O2(0)
    n_chunks = len(ORDER)
    for r in range(n_chunks):
        if r + 3 < n_chunks:
            O0(r + 3)
        if r + 2 < n_chunks:
            O1(r + 2)
        if r + 1 < n_chunks:
            O2(r + 1)
        if r == 1:
            W2()
        if r == 2:
            W4(0)
        if r == 4:
            W5(0)
        if r == 5:
            W1(1)
        if r == 6:
            W4(1)
        O3(r)
        T(r)
        if r - LAG >= 0:
            Pk(r - LAG)
    W5(1)
    for k in range(n_chunks):
        arrived(w_all.at[:, w_cols(k, 1)], wc_send.at[k], wc_recv.at[k])
    lax.fori_loop(0, 4, D, 0)
    Pk(6)
    lax.fori_loop(4, NT, D, 0)
    Pk(7)
    for cp in tile_out(NT - 2, (NT - 2) % 2) + tile_out(NT - 1, (NT - 1) % 2):
        cp.wait()
    for cp in sends:
        cp.wait_send()


def shards(out_grad, gate_pre, up_pre, down_weight):
    TB, D = out_grad.shape
    TOK, FFD = gate_pre.shape
    BLK = down_weight.shape[1]
    n = len(ORDER)
    any_spec = pl.BlockSpec(memory_space=pl.ANY)
    dma = pltpu.SemaphoreType.DMA
    flops = 4 * TOK * D * FFD
    return pl.pallas_call(
        kernel,
        out_shape=(
            jax.ShapeDtypeStruct((TOK, FFD), BF16),
            jax.ShapeDtypeStruct((TOK, FFD), BF16),
            jax.ShapeDtypeStruct((FFD, BLK), BF16),
        ),
        in_specs=[any_spec] * 4,
        out_specs=(any_spec,) * 3,
        scratch_shapes=[
            pltpu.VMEM((TOK, D), BF16),
            pltpu.VMEM((FFD, D), BF16),
            pltpu.VMEM((FFD, TOK), BF16),
            pltpu.VMEM((n, FFD, BLK), BF16),
            pltpu.VMEM((n, FFD, BLK), BF16),
            pltpu.VMEM((2, FFD, BLK), BF16),
            pltpu.VMEM((2, 2, FFD // 2, BLK), BF16),
            pltpu.VMEM((2, 2, FFD, BLK), BF16),
            pltpu.VMEM((FFD, BLK), BF16),
            pltpu.VMEM((TOK, BLK), F32),
            pltpu.VMEM((2, TOK, BLK), BF16),
            pltpu.VMEM((2, TOK, BLK), BF16),
            pltpu.VMEM((2, TOK, BLK), BF16),
            pltpu.VMEM((2, TOK, BLK), BF16),
            dma((n, 9)),
            dma((n, 9)),
            dma((14,)),
            dma((n, 2)),
            dma((n,)),
            dma((n,)),
            dma((n,)),
            dma((n,)),
            dma((2, 4)),
            dma((2, 4)),
            dma,
            dma,
            dma((n, 2)),
            dma,
            dma((2, 2)),
            dma((2, 2)),
            dma,
        ],
        compiler_params=pltpu.CompilerParams(
            collective_id=0, has_side_effects=True, vmem_limit_bytes=60 * 1024 * 1024
        ),
        cost_estimate=pl.CostEstimate(flops=flops, bytes_accessed=40 << 20, transcendentals=0),
    )(out_grad, gate_pre, up_pre, down_weight)


def solution(mesh):
    return jax.shard_map(
        shards,
        mesh=mesh,
        in_specs=(P(("dp", "mp"), None), P("dp", "mp"), P("dp", "mp"), P("mp", "dp")),
        out_specs=(P("dp", "mp"), P("dp", "mp"), P("mp", "dp")),
        check_vma=False,
    )
```

time: 383 us -> 171 us (0.45)
  waiting for transfers between devices: 317 us -> 0 us
  Pallas kernels: 0 us -> 160 us
  matrix products: 50.1 us -> 0 us
  between operations: 13.7 us -> 0.65 us
  local copies, waits for them, and re-layouts: 0 us -> 7.03 us
    all_gather x2 -> x0, waiting for transfers between devices: 178 us -> none  [the longest x1 113 us: shards(): full_rows = lax.all_gather(out_grad, 'mp', axis=0, tiled=True)]
    pallas_call x0 -> x1, Pallas kernels: none -> 160 us  [shards(): pl.pallas_call(kernel, out_shape=(jax.ShapeDtypeStruct((TOK, FFD), BF16),...]
    reduce_scatter x1 -> x0, waiting for transfers between devices: 137 us -> none  [shards(): lax.psum_scatter(lax.optimization_barrier(term.astype(jnp.bfloat16)).asty...]
    dot_general x2 -> x0, matrix products: 50.1 us -> none  [the longest x1 26.4 us: shards(): lax.dot_general(full_rows, lax.all_gather(down_weight, 'dp', axis=1, tile...]
    unnamed x0 -> x7, local copies, waits for them, and re-layouts: none -> 7.03 us
  transfers between devices with their start and end apart: 3 -> 0, of which waited for: 3 -> 0; matrix products, arithmetic and copies ran while one was open for 13% -> 0% of each run, Pallas kernels for 0% -> 0%
where the time goes in v1:
time: 171 us; the launch traced here: 168 us
  Pallas kernels  160 us (94%)
  local copies, waits for them, and re-layouts  7.03 us (4%)
    pallas_call x1, Pallas kernels, shards(): pl.pallas_call(kernel, out_shape=(jax.ShapeDtypeStruct((TOK, FFD), BF16),...  160 us
    unnamed x7, local copies, waits for them, and re-layouts  7.03 us

profile of v1, /device:TPU:0, one launch (start us, length us, event | category | flops | bytes accessed | tf_op | source)
XLA Modules:
  0.0 167.9 jit_solution(3764408094360788276)
XLA Ops:
  0.6 160.3 %shard_map.67 = (bf16[1024,1792]{1,0:T(8,128)(2,1)}, bf16[1024,1792]{1,0:T(8,128)(2,1)}, bf16[1792,256]{1,0:T(8,128)(2,1)}) custom-call(bf16[128,4096]{1,0:T(8,128)(2,1)} %og.1, bf16[1024,1792]{1,0:T(8,128)(2,1)} %gp.1, bf16[1024,1792]{1,0:T(8,128)(2,1)} %up.1, bf16[1792,256]{1,0:T(8,128)(2,1)} %w.1), custom_call_target="tpu_custom_call" | custom-call | flops 30064771072 | bytes 41943040 | tf_op jit(solution)/shard_map/pallas_call | solution.py:385
  160.9 0.0 copy-start
  160.9 4.3 %copy.10 = bf16[1024,1792]{1,0:T(8,128)(2,1)} copy(bf16[1024,1792]{1,0:T(8,128)(2,1)} %get-tuple-element.6) | data formatting | bytes 7340032
  165.2 0.0 copy-done
  165.2 0.0 copy-start.1
  165.2 1.8 %copy.11 = bf16[1024,1792]{1,0:T(8,128)(2,1)} copy(bf16[1024,1792]{1,0:T(8,128)(2,1)S(1)} %copy-done) | data formatting | bytes 7340032
  167.0 0.0 copy-done.1
  167.0 0.9 copy.12
Async XLA Ops:
  160.9 4.3 %copy-start = (bf16[1024,1792]{1,0:T(8,128)(2,1)S(1)}, bf16[1024,1792]{1,0:T(8,128)(2,1)}, u32[]{:S(2)}) copy-start(bf16[1024,1792]{1,0:T(8,128)(2,1)} %get-tuple-element.7) | copy-start | bytes 11010052
  165.2 1.8 %copy-start.1 = (bf16[1792,256]{1,0:T(8,128)(2,1)S(1)}, bf16[1792,256]{1,0:T(8,128)(2,1)}, u32[]{:S(2)}) copy-start(bf16[1792,256]{1,0:T(8,128)(2,1)} %get-tuple-element.8) | copy-start | bytes 2752516

commit v2 on v1

--- a/solution.py
+++ b/solution.py
@@ -1,3 +1,4 @@
+import itertools
 import math
 
 import jax
@@ -13,7 +14,20 @@
 
 ORDER = ((2, 1), (2, 0), (1, 1), (-1, 1), (1, 0), (-1, 0), (0, 1), (0, 0))
 SLOT = {at: k for k, at in enumerate(ORDER)}
-LAG = 2
+SPLIT = 832
+SCHEDULE = (
+    ("O0", 2), ("Wz", 0), ("O0", 0), ("O0", 3), ("Wz", 1), ("H", 0), ("O0", 1), ("H", 1), ("H", 2), ("Wy", 1),
+    ("O1b", 0), ("O1a", 2), ("O0", 4), ("Wy", 0), ("O1b", 2), ("O1a", 0), ("H", 3), ("O0", 6), ("O2", 0), ("Wp", 1),
+    ("H", 4), ("Wq", -1), ("H", 5), ("Wr", 0), ("O1b", 1), ("O3", 0), ("O1b", 6), ("H", 6), ("Wp", 0), ("O1a", 1),
+    ("O2", 1), ("O2", 2), ("T", 0), ("O1b", 3), ("Wq", 1), ("P", 0, 0), ("Ws", 0, 0), ("P", 0, 1), ("Ws", -1, 0),
+    ("O1a", 3), ("O3", 1), ("O0", 7), ("O2", 6), ("T", 1), ("O3", 2), ("P", 1, 1), ("O0", 5), ("Wr", 1), ("O2", 3),
+    ("O1a", 6), ("T", 2), ("Wq", 2), ("O1b", 4), ("Wc", 1), ("O1a", 4), ("P", 2, 1), ("Wy", 2), ("Wc", -1),
+    ("Ws", -1, 1), ("P", 1, 0), ("Ws", 1, 1), ("O3", 3), ("T", 3), ("O1b", 5), ("O2", 4), ("O3", 6), ("Ws", 2, 0),
+    ("P", 3, 1), ("P", 2, 0), ("O1a", 5), ("O2", 5), ("O3", 4), ("Ws", 1, 0), ("O1b", 7), ("T", 4), ("O3", 5),
+    ("T", 5), ("P", 3, 0), ("O1a", 7), ("Wc", 2), ("O2", 7), ("T", 6), ("P", 5, 1), ("Ws", 2, 1), ("P", 4, 1),
+    ("P", 5, 0), ("P", 4, 0), ("P", 6, 1), ("Wc", 0), ("Ws", 0, 1), ("O3", 7), ("T", 7), ("WD",), ("D", 0), ("D", 1),
+    ("D", 2), ("P", 6, 0), ("D", 3), ("D", 4), ("P", 7, 1), ("D", 5), ("D", 6), ("P", 7, 0),
+)
 
 
 def kernel(
@@ -104,56 +118,65 @@
 
     pl.semaphore_wait(barrier, 7)
 
-    def w_part(k, cc, part):
-        return w_all.at[pl.ds(part * HALF, HALF), w_cols(k, cc)]
-
-    def w_to(src, k, part, sem, to):
-        send(src, w_part(k, 0, part), w_send.at[sem], w_recv.at[k, part], to)
-
-    def w_got(k, part):
-        arrived(w_part(k, 0, part), w_send.at[0], w_recv.at[k, part])
-
-    def w_share(k):
-        send(
-            w_all.at[:, w_cols(k, 0)], w_all.at[:, w_cols(k, 1)], wc_send.at[k], wc_recv.at[k], CP
-        )
-
-    def W0():
-        a, b = w.at[pl.ds(0, HALF), :], w.at[pl.ds(HALF, HALF), :]
-        w_to(a, SLOT[-1, 0], 0, 0, ZP)
-        w_to(b, SLOT[1, 0], 1, 1, ZM)
-        w_to(a, SLOT[0, 1], 0, 2, YP)
-        w_to(b, SLOT[-1, 0], 1, 3, ZP)
-        w_to(a, SLOT[1, 0], 0, 4, ZM)
-        w_to(b, SLOT[0, 1], 1, 5, YP)
-
-    def W1(o):
-        w_got(SLOT[-1, o], 0)
-        w_to(w_part(SLOT[-1, o], 0, 0), SLOT[2, o], 0, 6 + 2 * o, ZP)
-        w_got(SLOT[1, o], 1)
-        w_to(w_part(SLOT[1, o], 0, 1), SLOT[2, o], 1, 7 + 2 * o, ZM)
-
-    def W2():
-        k = SLOT[0, 1]
-        w_got(k, 0)
-        w_to(w_part(k, 0, 0), SLOT[-1, 1], 0, 10, ZP)
-        w_to(w_part(k, 0, 0), SLOT[1, 1], 0, 11, ZM)
-        w_got(k, 1)
-        w_to(w_part(k, 0, 1), SLOT[1, 1], 1, 12, ZM)
-        w_to(w_part(k, 0, 1), SLOT[-1, 1], 1, 13, ZP)
-        w_share(k)
-
-    def W4(o):
-        w_got(SLOT[-1, o], 1)
-        w_share(SLOT[-1, o])
-        w_got(SLOT[1, o], 0)
-        w_share(SLOT[1, o])
-
-    def W5(o):
-        k = SLOT[2, o]
-        w_got(k, 0)
-        w_got(k, 1)
-        w_share(k)
+    def w_part(dz, o, part):
+        if o == 0:
+            rows = pl.ds(part * HALF, HALF)
+        elif part < 2:
+            rows = pl.ds(part * (SPLIT // 2), SPLIT // 2)
+        else:
+            rows = pl.ds(SPLIT, FFD - SPLIT)
+        return w_all.at[rows, w_cols(SLOT[dz, o], 0)]
+
+    n_w = itertools.count()
+
+    def w_to(src, dz, o, part, to):
+        send(src, w_part(dz, o, part), w_send.at[next(n_w)], w_recv.at[SLOT[dz, o], part], to)
+
+    w_seen = set()
+
+    def w_got(dz, o, part):
+        if (dz, o, part) not in w_seen:
+            w_seen.add((dz, o, part))
+            arrived(w_part(dz, o, part), w_send.at[0], w_recv.at[SLOT[dz, o], part])
+
+    def Wz(p):
+        w_to(w.at[pl.ds(p * HALF, HALF), :], -1, 0, p, ZP)
+        w_to(w.at[pl.ds((1 - p) * HALF, HALF), :], 1, 0, 1 - p, ZM)
+
+    def Wy(p):
+        rows = (pl.ds(0, SPLIT // 2), pl.ds(SPLIT // 2, SPLIT // 2), pl.ds(SPLIT, FFD - SPLIT))[p]
+        w_to(w.at[rows, :], 0, 1, p, YP)
+
+    def Wr(o):
+        w_got(-1, o, 0)
+        w_to(w_part(-1, o, 0), 2, o, 0, ZP)
+        w_got(1, o, 1)
+        w_to(w_part(1, o, 1), 2, o, 1, ZM)
+
+    def Wp(p):
+        w_got(0, 1, p)
+        for dz, to in ((-1, ZP), (1, ZM)) if p == 0 else ((1, ZM), (-1, ZP)):
+            w_to(w_part(0, 1, p), dz, 1, p, to)
+
+    def Wq(dz):
+        w_got(dz, 0, 0)
+        w_got(dz, 0, 1)
+        src = w_all.at[pl.ds(SPLIT, FFD - SPLIT), w_cols(SLOT[dz, 0], 0)]
+        w_to(src, dz, 1, 2, YP)
+
+    def Wc(dz):
+        for p in range(3):
+            w_got(dz, 1, p)
+
+    def Ws(dz, o):
+        k = SLOT[dz, o]
+        if (dz, o) == (0, 0):
+            w_own.wait()
+        send(w_all.at[:, w_cols(k, 0)], w_all.at[:, w_cols(k, 1)], wc_send.at[k], wc_recv.at[k], CP)
+
+    def WD():
+        for k in range(len(ORDER)):
+            arrived(w_all.at[:, w_cols(k, 1)], wc_send.at[k], wc_recv.at[k])
 
     def o_to(k, h, dx, part, kind, to):
         ref = o_all.at[o_rows(h, dx, part), o_cols(k)]
@@ -170,11 +193,13 @@
         o_to(k, 0, 0, None, 1, XP)
         o_to(k, 0, 0, None, 2, XM)
 
-    def O1(k):
+    def O1a(k):
         o_got(k, 0, -1, None, 1)
         o_to(k, 0, -1, 0, 3, XP)
         o_got(k, 0, 1, None, 2)
         o_to(k, 0, 1, 1, 4, XM)
+
+    def O1b(k):
         o_got(k, 1, 0, None, 0)
         o_to(k, 1, 0, None, 5, XP)
         o_to(k, 1, 0, None, 6, XM)
@@ -191,7 +216,7 @@
         o_got(k, 1, 2, 0, 7)
         o_got(k, 1, 2, 1, 8)
 
-    def hidden_tile(n, _):
+    def H(n):
         slot = n % 2
         for cp in tile_in(n, slot):
             cp.wait()
@@ -206,12 +231,13 @@
 
         lax.fori_loop(0, TOK // 128, rows, 0)
 
-        @pl.when(n + 2 < NT)
-        def _():
+        if n + 2 < NT:
             for cp in tile_in(n + 2, slot):
                 cp.start()
-
-        return 0
+        elif n == NT - 1:
+            for first in range(2):
+                for cp in tile_in(first, first):
+                    cp.start()
 
     def term(k, cc, dst):
         def rows(i, _):
@@ -234,55 +260,63 @@
         t_copies[k] = send(snd.at[slot], pre.at[k], t_send.at[k], t_recv.at[k], CP)
         term(k, 0, own.at[k])
 
-    def add(dst, others, start=0, size=None, scale=None):
+    def add(dst, parts, scale=None):
         step = 128
 
         def rows(i, _):
-            r = pl.ds(pl.multiple_of(start + i * step, step), step)
+            r = pl.ds(pl.multiple_of(i * step, step), step)
             total = dst[r, :].astype(F32)
-            for ref, at in others:
-                total += ref[pl.ds(pl.multiple_of(start - at + i * step, step), step), :].astype(F32)
+            for ref in parts:
+                total += ref[r, :].astype(F32)
             if scale is not None:
                 total *= scale
             dst[r, :] = total.astype(BF16)
             return 0
 
-        lax.fori_loop(0, size // step, rows, 0)
-
-    def Pk(k):
+        lax.fori_loop(0, HALF // step, rows, 0)
+
+    t_got = set()
+    gd_copies = []
+
+    def Pk(k, p):
         dz, o = ORDER[k]
-        blk = own.at[k]
-        arrived(pre.at[k], t_send.at[k], t_recv.at[k])
-        up_half, down_half = pl.ds(0, HALF), pl.ds(HALF, HALF)
+        rows = pl.ds(p * HALF, HALF)
+        blk = own.at[k, rows, :]
+        if k not in t_got:
+            arrived(pre.at[k], t_send.at[k], t_recv.at[k])
+            t_got.add(k)
+        parts = [pre.at[k, rows, :]]
+
+        def take(ref, sem):
+            arrived(ref, z_send.at[o, sem], z_recv.at[o, sem])
+            parts.append(ref)
+
         if dz == 2:
-            add(blk, [(pre.at[k], 0)], 0, FFD)
-            send(blk.at[up_half, :], half_in.at[o, 0], z_send.at[o, 0], z_recv.at[o, 0], ZP)
-            send(blk.at[down_half, :], half_in.at[o, 1], z_send.at[o, 1], z_recv.at[o, 1], ZM)
-        elif dz == 1:
-            add(blk, [(pre.at[k], 0)], HALF, HALF)
-            arrived(half_in.at[o, 0], z_send.at[o, 0], z_recv.at[o, 0])
-            add(blk, [(pre.at[k], 0), (half_in.at[o, 0], 0)], 0, HALF)
-            send(blk, full_in.at[o, 0], z_send.at[o, 2], z_recv.at[o, 2], ZP)
-        elif dz == -1:
-            add(blk, [(pre.at[k], 0)], 0, HALF)
-            arrived(half_in.at[o, 1], z_send.at[o, 1], z_recv.at[o, 1])
-            add(blk, [(pre.at[k], 0), (half_in.at[o, 1], HALF)], HALF, HALF)
-            send(blk, full_in.at[o, 1], z_send.at[o, 3], z_recv.at[o, 3], ZM)
+            add(blk, parts)
+            send(blk, half_in.at[o, p], z_send.at[o, p], z_recv.at[o, p], (ZP, ZM)[p])
+        elif dz:
+            side = 0 if dz == 1 else 1
+            if p == side:
+                take(half_in.at[o, p], p)
+            add(blk, parts)
+            sem = 2 + 2 * side + p
+            dst = full_in.at[o, side, rows, :]
+            send(blk, dst, z_send.at[o, sem], z_recv.at[o, sem], (ZP, ZM)[side])
         else:
-            arrived(full_in.at[o, 0], z_send.at[o, 2], z_recv.at[o, 2])
-            arrived(full_in.at[o, 1], z_send.at[o, 3], z_recv.at[o, 3])
-            parts = [(pre.at[k], 0), (full_in.at[o, 0], 0), (full_in.at[o, 1], 0)]
+            for side in range(2):
+                take(full_in.at[o, side, rows, :], 2 + 2 * side + p)
             if o == 1:
-                add(blk, parts, 0, FFD)
-                send(blk, y_in, y_send, y_recv, YP)
+                add(blk, parts)
+                send(blk, y_in.at[rows, :], y_send.at[p], y_recv.at[p], YP)
             else:
-                arrived(y_in, y_send, y_recv)
-                add(blk, parts + [(y_in, 0)], 0, FFD, norm)
-                cp = pltpu.make_async_copy(blk, gd, gd_sem)
+                arrived(y_in.at[rows, :], y_send.at[p], y_recv.at[p])
+                parts.append(y_in.at[rows, :])
+                add(blk, parts, norm)
+                cp = pltpu.make_async_copy(blk, gd.at[rows, :], gd_sem.at[p])
                 cp.start()
-                cp.wait()
-
-    def D(n, _):
+                gd_copies.append(cp)
+
+    def D(n):
         slot = n % 2
 
         def mm(i, _):
@@ -299,8 +333,7 @@
         for cp in tile_in(n, slot):
             cp.wait()
 
-        @pl.when(n >= 2)
-        def _():
+        if n >= 2:
             for cp in tile_out(n - 2, slot):
                 cp.wait()
 
@@ -317,58 +350,19 @@
         lax.fori_loop(0, TOK // 64, rows, 0)
         for cp in tile_out(n, slot):
             cp.start()
-
-        @pl.when(n + 2 < NT)
-        def _():
+        if n + 2 < NT:
             for cp in tile_in(n + 2, slot):
                 cp.start()
 
-        return 0
-
-    W0()
-    O0(0)
-    O0(1)
-    O0(2)
-    lax.fori_loop(0, NT, hidden_tile, 0)
-    for slot in range(2):
-        for cp in tile_in(slot, slot):
-            cp.start()
-    w_own.wait()
-    w_share(SLOT[0, 0])
-    O1(0)
-    W1(0)
-    O1(1)
-    O2(0)
-    n_chunks = len(ORDER)
-    for r in range(n_chunks):
-        if r + 3 < n_chunks:
-            O0(r + 3)
-        if r + 2 < n_chunks:
-            O1(r + 2)
-        if r + 1 < n_chunks:
-            O2(r + 1)
-        if r == 1:
-            W2()
-        if r == 2:
-            W4(0)
-        if r == 4:
-            W5(0)
-        if r == 5:
-            W1(1)
-        if r == 6:
-            W4(1)
-        O3(r)
-        T(r)
-        if r - LAG >= 0:
-            Pk(r - LAG)
-    W5(1)
-    for k in range(n_chunks):
-        arrived(w_all.at[:, w_cols(k, 1)], wc_send.at[k], wc_recv.at[k])
-    lax.fori_loop(0, 4, D, 0)
-    Pk(6)
-    lax.fori_loop(4, NT, D, 0)
-    Pk(7)
+    tasks = dict(
+        O0=O0, O1a=O1a, O1b=O1b, O2=O2, O3=O3, H=H, T=T, P=Pk, D=D,
+        Wz=Wz, Wy=Wy, Wr=Wr, Wp=Wp, Wq=Wq, Wc=Wc, Ws=Ws, WD=WD,
+    )
+    for name, *at in SCHEDULE:
+        tasks[name](*at)
     for cp in tile_out(NT - 2, (NT - 2) % 2) + tile_out(NT - 1, (NT - 1) % 2):
+        cp.wait()
+    for cp in gd_copies:
         cp.wait()
     for cp in sends:
         cp.wait_send()
@@ -408,21 +402,21 @@
             pltpu.VMEM((2, TOK, BLK), BF16),
             dma((n, 9)),
             dma((n, 9)),
-            dma((14,)),
-            dma((n, 2)),
+            dma((18,)),
+            dma((n, 3)),
             dma((n,)),
             dma((n,)),
             dma((n,)),
             dma((n,)),
-            dma((2, 4)),
-            dma((2, 4)),
-            dma,
-            dma,
+            dma((2, 6)),
+            dma((2, 6)),
+            dma((2,)),
+            dma((2,)),
             dma((n, 2)),
             dma,
             dma((2, 2)),
             dma((2, 2)),
-            dma,
+            dma((2,)),
         ],
         compiler_params=pltpu.CompilerParams(
             collective_id=0, has_side_effects=True, vmem_limit_bytes=60 * 1024 * 1024

time: 171 us -> 122 us (0.71); the launches traced: 168 us -> 122 us
  Pallas kernels: 160 us -> 114 us
    pallas_call x1, Pallas kernels: 160 us -> 114 us  [shards(): pl.pallas_call(kernel, out_shape=(jax.ShapeDtypeStruct((TOK, FFD), BF16),...]
where the time goes in v2:
time: 122 us
  Pallas kernels  114 us (93%)
  local copies, waits for them, and re-layouts  7.03 us (6%)
    pallas_call x1, Pallas kernels, shards(): pl.pallas_call(kernel, out_shape=(jax.ShapeDtypeStruct((TOK, FFD), BF16),...  114 us
    unnamed x7, local copies, waits for them, and re-layouts  7.03 us

profile of v2, /device:TPU:0, one launch (start us, length us, event | category | flops | bytes accessed | tf_op | source)
XLA Modules:
  0.0 121.7 jit_solution(15940969834604171549)
XLA Ops:
  0.6 114.0 %shard_map.67 = (bf16[1024,1792]{1,0:T(8,128)(2,1)}, bf16[1024,1792]{1,0:T(8,128)(2,1)}, bf16[1792,256]{1,0:T(8,128)(2,1)}) custom-call(bf16[128,4096]{1,0:T(8,128)(2,1)} %og.1, bf16[1024,1792]{1,0:T(8,128)(2,1)} %gp.1, bf16[1024,1792]{1,0:T(8,128)(2,1)} %up.1, bf16[1792,256]{1,0:T(8,128)(2,1)} %w.1), custom_call_target="tpu_custom_call" | custom-call | flops 30064771072 | bytes 41943040 | tf_op jit(solution)/shard_map/pallas_call | solution.py:379
  114.7 0.0 copy-start
  114.7 4.3 %copy.10 = bf16[1024,1792]{1,0:T(8,128)(2,1)} copy(bf16[1024,1792]{1,0:T(8,128)(2,1)} %get-tuple-element.6) | data formatting | bytes 7340032
  118.9 0.0 copy-done
  118.9 0.0 copy-start.1
  118.9 1.8 %copy.11 = bf16[1024,1792]{1,0:T(8,128)(2,1)} copy(bf16[1024,1792]{1,0:T(8,128)(2,1)S(1)} %copy-done) | data formatting | bytes 7340032
  120.8 0.0 copy-done.1
  120.8 0.9 copy.12
Async XLA Ops:
  114.7 4.3 %copy-start = (bf16[1024,1792]{1,0:T(8,128)(2,1)S(1)}, bf16[1024,1792]{1,0:T(8,128)(2,1)}, u32[]{:S(2)}) copy-start(bf16[1024,1792]{1,0:T(8,128)(2,1)} %get-tuple-element.7) | copy-start | bytes 11010052
  118.9 1.8 %copy-start.1 = (bf16[1792,256]{1,0:T(8,128)(2,1)S(1)}, bf16[1792,256]{1,0:T(8,128)(2,1)}, u32[]{:S(2)}) copy-start(bf16[1792,256]{1,0:T(8,128)(2,1)} %get-tuple-element.8) | copy-start | bytes 2752516

commit v3 on v2

--- a/solution.py
+++ b/solution.py
@@ -1,3 +1,4 @@
+import functools
 import itertools
 import math
 
@@ -14,27 +15,30 @@
 
 ORDER = ((2, 1), (2, 0), (1, 1), (-1, 1), (1, 0), (-1, 0), (0, 1), (0, 0))
 SLOT = {at: k for k, at in enumerate(ORDER)}
-SPLIT = 832
+SPLIT = 1088
+SPLIT2 = 1408
+VMEM_LIMIT = 51 << 20
 SCHEDULE = (
-    ("O0", 2), ("Wz", 0), ("O0", 0), ("O0", 3), ("Wz", 1), ("H", 0), ("O0", 1), ("H", 1), ("H", 2), ("Wy", 1),
-    ("O1b", 0), ("O1a", 2), ("O0", 4), ("Wy", 0), ("O1b", 2), ("O1a", 0), ("H", 3), ("O0", 6), ("O2", 0), ("Wp", 1),
-    ("H", 4), ("Wq", -1), ("H", 5), ("Wr", 0), ("O1b", 1), ("O3", 0), ("O1b", 6), ("H", 6), ("Wp", 0), ("O1a", 1),
-    ("O2", 1), ("O2", 2), ("T", 0), ("O1b", 3), ("Wq", 1), ("P", 0, 0), ("Ws", 0, 0), ("P", 0, 1), ("Ws", -1, 0),
-    ("O1a", 3), ("O3", 1), ("O0", 7), ("O2", 6), ("T", 1), ("O3", 2), ("P", 1, 1), ("O0", 5), ("Wr", 1), ("O2", 3),
-    ("O1a", 6), ("T", 2), ("Wq", 2), ("O1b", 4), ("Wc", 1), ("O1a", 4), ("P", 2, 1), ("Wy", 2), ("Wc", -1),
-    ("Ws", -1, 1), ("P", 1, 0), ("Ws", 1, 1), ("O3", 3), ("T", 3), ("O1b", 5), ("O2", 4), ("O3", 6), ("Ws", 2, 0),
-    ("P", 3, 1), ("P", 2, 0), ("O1a", 5), ("O2", 5), ("O3", 4), ("Ws", 1, 0), ("O1b", 7), ("T", 4), ("O3", 5),
-    ("T", 5), ("P", 3, 0), ("O1a", 7), ("Wc", 2), ("O2", 7), ("T", 6), ("P", 5, 1), ("Ws", 2, 1), ("P", 4, 1),
-    ("P", 5, 0), ("P", 4, 0), ("P", 6, 1), ("Wc", 0), ("Ws", 0, 1), ("O3", 7), ("T", 7), ("WD",), ("D", 0), ("D", 1),
-    ("D", 2), ("P", 6, 0), ("D", 3), ("D", 4), ("P", 7, 1), ("D", 5), ("D", 6), ("P", 7, 0),
+    ("Wz", 0), ("O0", 0), ("O0", 3), ("Ws", 0, 0), ("O0", 2), ("O0", 1), ("H", 0), ("Wy", 0), ("Wy", 1), ("Wz", 1),
+    ("Wy", 2), ("H", 1), ("H", 2), ("O1b", 0), ("O1a", 0), ("O1b", 1), ("Wr", 0), ("O2", 0), ("O0", 4), ("O2", 1),
+    ("H", 3), ("O0", 5), ("O1b", 2), ("Wp", 0), ("H", 4), ("H", 5), ("H", 6), ("O3", 0), ("Wp", 1), ("O1a", 1),
+    ("T", 0), ("O0", 6), ("O1b", 3), ("Wq", 2), ("PY", 0), ("O3", 1), ("O2", 2), ("O1a", 3), ("O1a", 2), ("O2", 3),
+    ("O1b", 4), ("P", 0, 1), ("O1b", 5), ("P", 0, 0), ("O1a", 4), ("O0", 7), ("T", 1), ("Wc", 0), ("Wr", 1),
+    ("O1a", 5), ("O3", 3), ("O3", 2), ("Wq", -1), ("Ws", 2, 0), ("P", 1, 0), ("Wq", 1), ("T", 2), ("O2", 4),
+    ("O1b", 6), ("T", 3), ("P", 1, 1), ("O2", 5), ("P", 3, 0), ("P", 2, 0), ("PY", 3), ("Wc", 2), ("Ws", 0, 1),
+    ("PY", 2), ("O3", 4), ("Ws", 2, 1), ("P", 2, 1), ("P", 3, 1), ("Ws", -1, 0), ("O1b", 7), ("T", 4), ("O1a", 6),
+    ("O2", 6), ("O3", 5), ("Ws", 1, 0), ("O1a", 7), ("Wc", -1), ("Ws", -1, 1), ("T", 5), ("P", 4, 0), ("O2", 7),
+    ("O3", 6), ("T", 6), ("P", 5, 0), ("O3", 7), ("Wc", 1), ("Ws", 1, 1), ("T", 7), ("P", 6, 0), ("WD",), ("D", 0),
+    ("PY", 6), ("P", 5, 1), ("D", 1), ("P", 6, 1), ("Z", 0), ("P", 4, 1), ("D", 2), ("D", 3), ("D", 4), ("D", 5),
+    ("D", 6), ("Z", 1),
 )
 
 
 def kernel(
-    og, gp, up, w, gg, gu, gd,
-    o_all, w_all, h_t, own, pre, snd, half_in, full_in, y_in, acc, gbuf, ubuf, ggbuf, gubuf,
+    og, gp, up, w, gg, gu, last, up_in, down_in, y_in,
+    o_all, w_all, h_t, own, pre, snd, half_in, full_in, y_early, acc, gbuf, ubuf, ggbuf, gubuf,
     o_send, o_recv, w_send, w_recv, wc_send, wc_recv, t_send, t_recv, z_send, z_recv, y_send, y_recv,
-    o_local, w_local, in_sem, out_sem, gd_sem,
+    o_local, w_local, in_sem, out_sem, last_sem,
 ):
     TB = og.shape[0]
     BLK = w.shape[1]
@@ -43,7 +47,6 @@
     HALF = FFD // 2
     TH = TB // 2
     NT = FFD // BLK
-    norm = 1.0 / math.sqrt(TOK * 16)
 
     dp = lax.axis_index("dp")
     mp = lax.axis_index("mp")
@@ -260,61 +263,108 @@
         t_copies[k] = send(snd.at[slot], pre.at[k], t_send.at[k], t_recv.at[k], CP)
         term(k, 0, own.at[k])
 
-    def add(dst, parts, scale=None):
-        step = 128
-
-        def rows(i, _):
-            r = pl.ds(pl.multiple_of(i * step, step), step)
-            total = dst[r, :].astype(F32)
-            for ref in parts:
-                total += ref[r, :].astype(F32)
-            if scale is not None:
-                total *= scale
-            dst[r, :] = total.astype(BF16)
-            return 0
-
-        lax.fori_loop(0, HALF // step, rows, 0)
-
-    t_got = set()
-    gd_copies = []
+    def row_part(o, p):
+        if o == 0:
+            return p * HALF, HALF
+        return (p * (SPLIT2 // 2), SPLIT2 // 2) if p < 2 else (SPLIT2, FFD - SPLIT2)
+
+    def add(k, at, size, others):
+        step = 64
+        others = [(pre.at[k], 0, FFD), *others]
+        cuts = {at, at + size}
+        for _, first, many in others:
+            cuts |= {row for row in (first, first + many) if at < row < at + size}
+        cuts = sorted(cuts)
+        for low, high in zip(cuts, cuts[1:]):
+            inside = [(ref, first) for ref, first, many in others if first <= low and high <= first + many]
+
+            def rows(i, _, low=low, inside=inside):
+                r = pl.ds(pl.multiple_of(low + i * step, step), step)
+                total = own[k, r, :].astype(F32)
+                for ref, first in inside:
+                    total += ref[pl.ds(pl.multiple_of(low - first + i * step, step), step), :].astype(F32)
+                own[k, r, :] = total.astype(BF16)
+                return 0
+
+            lax.fori_loop(0, (high - low) // step, rows, 0)
+
+    seen = set()
+    last_copies = []
+
+    def once(ref, ss, rs, *name):
+        if name not in seen:
+            seen.add(name)
+            arrived(ref, ss, rs)
+
+    def y_part(dz, p):
+        if dz == 0:
+            at, size = row_part(1, p)
+            return y_in.at[pl.ds(at, size), :], p
+        i = (2, 1, -1).index(dz)
+        return y_early.at[i], 3 + i
+
+    def y_got(dz, p):
+        ref, sem = y_part(dz, p)
+        once(ref, y_send.at[sem], y_recv.at[sem], "y", sem)
+
+    def y_to(k, dz, p):
+        at, size = row_part(1, p)
+        ref, sem = y_part(dz, p)
+        send(own.at[k, pl.ds(at, size), :], ref, y_send.at[sem], y_recv.at[sem], YP)
+
+    def PY(k):
+        once(pre.at[k], t_send.at[k], t_recv.at[k], "t", k)
+        at, size = row_part(1, 2)
+        add(k, at, size, [])
+        y_to(k, ORDER[k][0], 2)
 
     def Pk(k, p):
         dz, o = ORDER[k]
-        rows = pl.ds(p * HALF, HALF)
+        at, size = row_part(o, p)
+        rows = pl.ds(at, size)
         blk = own.at[k, rows, :]
-        if k not in t_got:
-            arrived(pre.at[k], t_send.at[k], t_recv.at[k])
-            t_got.add(k)
-        parts = [pre.at[k, rows, :]]
-
-        def take(ref, sem):
-            arrived(ref, z_send.at[o, sem], z_recv.at[o, sem])
-            parts.append(ref)
-
+        once(pre.at[k], t_send.at[k], t_recv.at[k], "t", k)
+        others = []
+        if o == 0 and dz and p == 1:
+            y_got(dz, 2)
+            others.append((y_part(dz, 2)[0], SPLIT2, FFD - SPLIT2))
         if dz == 2:
-            add(blk, parts)
-            send(blk, half_in.at[o, p], z_send.at[o, p], z_recv.at[o, p], (ZP, ZM)[p])
+            add(k, at, size, others)
+            send(blk, half_in.at[o, p, pl.ds(0, size), :], z_send.at[o, p], z_recv.at[o, p], (ZP, ZM)[p])
         elif dz:
             side = 0 if dz == 1 else 1
             if p == side:
-                take(half_in.at[o, p], p)
-            add(blk, parts)
+                ref = half_in.at[o, p, pl.ds(0, size), :]
+                arrived(ref, z_send.at[o, p], z_recv.at[o, p])
+                others.append((ref, at, size))
+            add(k, at, size, others)
             sem = 2 + 2 * side + p
-            dst = full_in.at[o, side, rows, :]
+            dst = full_in.at[side, rows, :] if o else (up_in, down_in)[side].at[rows, :]
             send(blk, dst, z_send.at[o, sem], z_recv.at[o, sem], (ZP, ZM)[side])
         else:
             for side in range(2):
-                take(full_in.at[o, side, rows, :], 2 + 2 * side + p)
-            if o == 1:
-                add(blk, parts)
-                send(blk, y_in.at[rows, :], y_send.at[p], y_recv.at[p], YP)
-            else:
-                arrived(y_in.at[rows, :], y_send.at[p], y_recv.at[p])
-                parts.append(y_in.at[rows, :])
-                add(blk, parts, norm)
-                cp = pltpu.make_async_copy(blk, gd.at[rows, :], gd_sem.at[p])
-                cp.start()
-                gd_copies.append(cp)
+                sem = 2 + 2 * side + p
+                arrived(full_in.at[side, rows, :], z_send.at[o, sem], z_recv.at[o, sem])
+                others.append((full_in.at[side], 0, FFD))
+            add(k, at, size, others)
+            y_to(k, 0, p)
+
+    def Z(p):
+        k = SLOT[0, 0]
+        if p == 0:
+            once(pre.at[k], t_send.at[k], t_recv.at[k], "t", k)
+            add(k, 0, FFD, [])
+            cp = pltpu.make_async_copy(own.at[k], last, last_sem)
+            cp.start()
+            last_copies.append(cp)
+            return
+        for half in range(2):
+            rows = pl.ds(half * HALF, HALF)
+            for side, ref in enumerate((up_in, down_in)):
+                sem = 2 + 2 * side + half
+                arrived(ref.at[rows, :], z_send.at[0, sem], z_recv.at[0, sem])
+        for part in range(3):
+            y_got(0, part)
 
     def D(n):
         slot = n % 2
@@ -355,17 +405,37 @@
                 cp.start()
 
     tasks = dict(
-        O0=O0, O1a=O1a, O1b=O1b, O2=O2, O3=O3, H=H, T=T, P=Pk, D=D,
+        O0=O0, O1a=O1a, O1b=O1b, O2=O2, O3=O3, H=H, T=T, P=Pk, PY=PY, Z=Z, D=D,
         Wz=Wz, Wy=Wy, Wr=Wr, Wp=Wp, Wq=Wq, Wc=Wc, Ws=Ws, WD=WD,
     )
     for name, *at in SCHEDULE:
         tasks[name](*at)
     for cp in tile_out(NT - 2, (NT - 2) % 2) + tile_out(NT - 1, (NT - 1) % 2):
         cp.wait()
-    for cp in gd_copies:
+    for cp in last_copies:
         cp.wait()
     for cp in sends:
         cp.wait_send()
+
+
+def finish(norm, gg_in, gu_in, last, up_in, down_in, y_in, gg, gu, gd, total, sem):
+    copies = [pltpu.make_async_copy(src, dst, sem.at[i]) for i, (src, dst) in enumerate(((gg_in, gg), (gu_in, gu)))]
+    for cp in copies:
+        cp.start()
+
+    def rows(i, _):
+        r = pl.ds(pl.multiple_of(i * 128, 128), 128)
+        acc = last[r, :].astype(F32)
+        for ref in (up_in, down_in, y_in):
+            acc += ref[r, :].astype(F32)
+        total[r, :] = (acc * norm).astype(BF16)
+        return 0
+
+    lax.fori_loop(0, total.shape[0] // 128, rows, 0)
+    copies.append(pltpu.make_async_copy(total, gd, sem.at[2]))
+    copies[-1].start()
+    for cp in copies:
+        cp.wait()
 
 
 def shards(out_grad, gate_pre, up_pre, down_weight):
@@ -376,15 +446,11 @@
     any_spec = pl.BlockSpec(memory_space=pl.ANY)
     dma = pltpu.SemaphoreType.DMA
     flops = 4 * TOK * D * FFD
-    return pl.pallas_call(
+    results = pl.pallas_call(
         kernel,
-        out_shape=(
-            jax.ShapeDtypeStruct((TOK, FFD), BF16),
-            jax.ShapeDtypeStruct((TOK, FFD), BF16),
-            jax.ShapeDtypeStruct((FFD, BLK), BF16),
-        ),
+        out_shape=[pltpu.VMEM((TOK, FFD), BF16)] * 2 + [pltpu.VMEM((FFD, BLK), BF16)] * 4,
         in_specs=[any_spec] * 4,
-        out_specs=(any_spec,) * 3,
+        out_specs=[any_spec] * 6,
         scratch_shapes=[
             pltpu.VMEM((TOK, D), BF16),
             pltpu.VMEM((FFD, D), BF16),
@@ -393,8 +459,8 @@
             pltpu.VMEM((n, FFD, BLK), BF16),
             pltpu.VMEM((2, FFD, BLK), BF16),
             pltpu.VMEM((2, 2, FFD // 2, BLK), BF16),
-            pltpu.VMEM((2, 2, FFD, BLK), BF16),
-            pltpu.VMEM((FFD, BLK), BF16),
+            pltpu.VMEM((2, FFD, BLK), BF16),
+            pltpu.VMEM((3, FFD - SPLIT2, BLK), BF16),
             pltpu.VMEM((TOK, BLK), F32),
             pltpu.VMEM((2, TOK, BLK), BF16),
             pltpu.VMEM((2, TOK, BLK), BF16),
@@ -410,19 +476,27 @@
             dma((n,)),
             dma((2, 6)),
             dma((2, 6)),
-            dma((2,)),
-            dma((2,)),
+            dma((6,)),
+            dma((6,)),
             dma((n, 2)),
             dma,
             dma((2, 2)),
             dma((2, 2)),
-            dma((2,)),
+            dma,
         ],
         compiler_params=pltpu.CompilerParams(
-            collective_id=0, has_side_effects=True, vmem_limit_bytes=60 * 1024 * 1024
+            collective_id=0, has_side_effects=True, vmem_limit_bytes=VMEM_LIMIT
         ),
         cost_estimate=pl.CostEstimate(flops=flops, bytes_accessed=40 << 20, transcendentals=0),
     )(out_grad, gate_pre, up_pre, down_weight)
+    return pl.pallas_call(
+        functools.partial(finish, 1.0 / math.sqrt(TOK * lax.axis_size("dp"))),
+        out_shape=[jax.ShapeDtypeStruct(shape, BF16) for shape in ((TOK, FFD), (TOK, FFD), (FFD, BLK))],
+        in_specs=[any_spec] * 2 + [pl.BlockSpec(memory_space=pltpu.VMEM)] * 4,
+        out_specs=[any_spec] * 3,
+        scratch_shapes=[pltpu.VMEM((FFD, BLK), BF16), dma((3,))],
+        compiler_params=pltpu.CompilerParams(vmem_limit_bytes=2 << 20),
+    )(*(pltpu.with_memory_space_constraint(a, pltpu.VMEM) for a in results))
 
 
 def solution(mesh):

time: 122 us -> 115 us (0.943)
  local copies, waits for them, and re-layouts: 7.03 us -> 0 us
    unnamed x7 -> x0, local copies, waits for them, and re-layouts: 7.03 us -> none
    pallas_call x1 -> x2, Pallas kernels: 114 us -> 114 us  [the longest x1 111 us: shards(): pl.pallas_call(kernel, out_shape=[pltpu.VMEM((TOK, FFD), BF16)] * 2 + [pl...]
where the time goes in v3:
time: 115 us
  Pallas kernels  114 us (99%)
    pallas_call x1, Pallas kernels, shards(): pl.pallas_call(kernel, out_shape=[pltpu.VMEM((TOK, FFD), BF16)] * 2 + [pl...  111 us
    pallas_call x1, Pallas kernels, shards(): pl.pallas_call(functools.partial(finish, 1.0 / math.sqrt(TOK * lax.axis_s...  3.37 us

profile of v3, /device:TPU:0, one launch (start us, length us, event | category | flops | bytes accessed | tf_op | source)
XLA Modules:
  0.0 115.0 jit_solution(15389639157234154994)
XLA Ops:
  0.6 110.9 %shard_map.67 = (bf16[1024,1792]{1,0:T(8,128)(2,1)S(1)}, bf16[1024,1792]{1,0:T(8,128)(2,1)S(1)}, bf16[1792,256]{1,0:T(8,128)(2,1)S(1)}, bf16[1792,256]{1,0:T(8,1...) custom-call(bf16[128,4096]{1,0:T(8,128)(2,1)} %og.1, bf16[1024,1792]{1,0:T(8,128)(2,1)} %gp.1, ...), custom_call_target="tpu_custom_call" | custom-call | flops 30064771072 | bytes 41943040 | tf_op jit(solution)/shard_map/pallas_call | solution.py:449
  111.5 3.4 %shard_map.68 = (bf16[1024,1792]{1,0:T(8,128)(2,1)}, bf16[1024,1792]{1,0:T(8,128)(2,1)}, bf16[1792,256]{1,0:T(8,128)(2,1)}) custom-call(bf16[1024,1792]{1,0:T(8,128)(2,1)S(1)} %get-tuple-element.9.gg_in, bf16[1024,1792]{1,0:T(8,128)(2,1)S(1)} %get-tuple-element.10.gu_in, bf16[1792,256]{1,0:T(8,128)(2,1)S(1)} %get-tuple-element.11.last, ...), custom_call_target="tpu_custom_call" | custom-call | tf_op jit(solution)/shard_map/pallas_call | solution.py:492

commit v4 on v3

--- a/solution.py
+++ b/solution.py
@@ -1,5 +1,4 @@
 import functools
-import itertools
 import math
 
 import jax
@@ -15,21 +14,26 @@
 
 ORDER = ((2, 1), (2, 0), (1, 1), (-1, 1), (1, 0), (-1, 0), (0, 1), (0, 0))
 SLOT = {at: k for k, at in enumerate(ORDER)}
-SPLIT = 1088
-SPLIT2 = 1408
+W_GROUPS = (
+    ((-1, 0, 0), (1, 0, 1)), ((-1, 0, 1),), ((1, 0, 0),), ((2, 0, 0), (2, 0, 1)), ((0, 1, 0),), ((0, 1, 1),), ((0, 1, 2),),
+    ((-1, 1, 0), (1, 1, 1)), ((-1, 1, 1), (-1, 1, 2)), ((1, 1, 0), (1, 1, 2)), ((2, 1, 0), (2, 1, 1), (2, 1, 2)),
+)
+SPLIT = 1184
+SPLIT2 = 1280
+FIRST = 1
 VMEM_LIMIT = 51 << 20
 SCHEDULE = (
-    ("Wz", 0), ("O0", 0), ("O0", 3), ("Ws", 0, 0), ("O0", 2), ("O0", 1), ("H", 0), ("Wy", 0), ("Wy", 1), ("Wz", 1),
-    ("Wy", 2), ("H", 1), ("H", 2), ("O1b", 0), ("O1a", 0), ("O1b", 1), ("Wr", 0), ("O2", 0), ("O0", 4), ("O2", 1),
-    ("H", 3), ("O0", 5), ("O1b", 2), ("Wp", 0), ("H", 4), ("H", 5), ("H", 6), ("O3", 0), ("Wp", 1), ("O1a", 1),
-    ("T", 0), ("O0", 6), ("O1b", 3), ("Wq", 2), ("PY", 0), ("O3", 1), ("O2", 2), ("O1a", 3), ("O1a", 2), ("O2", 3),
-    ("O1b", 4), ("P", 0, 1), ("O1b", 5), ("P", 0, 0), ("O1a", 4), ("O0", 7), ("T", 1), ("Wc", 0), ("Wr", 1),
-    ("O1a", 5), ("O3", 3), ("O3", 2), ("Wq", -1), ("Ws", 2, 0), ("P", 1, 0), ("Wq", 1), ("T", 2), ("O2", 4),
-    ("O1b", 6), ("T", 3), ("P", 1, 1), ("O2", 5), ("P", 3, 0), ("P", 2, 0), ("PY", 3), ("Wc", 2), ("Ws", 0, 1),
-    ("PY", 2), ("O3", 4), ("Ws", 2, 1), ("P", 2, 1), ("P", 3, 1), ("Ws", -1, 0), ("O1b", 7), ("T", 4), ("O1a", 6),
-    ("O2", 6), ("O3", 5), ("Ws", 1, 0), ("O1a", 7), ("Wc", -1), ("Ws", -1, 1), ("T", 5), ("P", 4, 0), ("O2", 7),
-    ("O3", 6), ("T", 6), ("P", 5, 0), ("O3", 7), ("Wc", 1), ("Ws", 1, 1), ("T", 7), ("P", 6, 0), ("WD",), ("D", 0),
-    ("PY", 6), ("P", 5, 1), ("D", 1), ("P", 6, 1), ("Z", 0), ("P", 4, 1), ("D", 2), ("D", 3), ("D", 4), ("D", 5),
+    ("Wz", 0), ("O0", 1), ("O0", 3), ("O0", 0), ("H", 0), ("H", 1), ("Wz", 1), ("O0", 2), ("O1b", 3), ("Wy", 0),
+    ("Wy", 1), ("O1b", 0), ("O1b", 1), ("O1a", 3), ("H", 2), ("O1a", 0), ("Wr", 0), ("O2", 0), ("Wy", 2), ("O2", 1),
+    ("O1a", 2), ("H", 3), ("O2", 3), ("H", 4), ("H", 5), ("O1a", 1), ("O3", 0), ("Wp", 0), ("O1b", 2), ("Wp", 1),
+    ("O0", 5), ("O0", 4), ("H", 6), ("T", 0), ("P", 0, 1), ("O3", 1), ("O0", 6), ("PY", 0), ("Wc", 0), ("O0", 7),
+    ("Ws", 0, 1), ("T", 1), ("O2", 2), ("P", 0, 0), ("O1b", 5), ("Wq", 2), ("Ws", 0, 0), ("O3", 3), ("Wr", 1),
+    ("O1b", 4), ("T", 3), ("P", 1, 0), ("Wq", -1), ("O1a", 5), ("O3", 2), ("P", 1, 1), ("O1b", 6), ("T", 2),
+    ("Ws", 2, 0), ("O2", 5), ("Wq", 1), ("O2", 4), ("O1a", 4), ("Ws", -1, 0), ("P", 2, 1), ("O1b", 7), ("P", 3, 1),
+    ("O1a", 6), ("Ws", 1, 0), ("PY", 3), ("Wc", 2), ("PY", 2), ("P", 3, 0), ("O3", 5), ("O2", 6), ("Ws", 2, 1),
+    ("O1a", 7), ("T", 5), ("O3", 4), ("T", 4), ("P", 2, 0), ("Wc", -1), ("O2", 7), ("P", 5, 0), ("O3", 6),
+    ("Ws", -1, 1), ("T", 6), ("Wc", 1), ("O3", 7), ("Ws", 1, 1), ("T", 7), ("P", 4, 0), ("PY", 6), ("WD",), ("D", 0),
+    ("D", 1), ("P", 6, 1), ("P", 4, 1), ("D", 2), ("P", 5, 1), ("P", 6, 0), ("Z", 0), ("D", 3), ("D", 4), ("D", 5),
     ("D", 6), ("Z", 1),
 )
 
@@ -37,7 +41,7 @@
 def kernel(
     og, gp, up, w, gg, gu, last, up_in, down_in, y_in,
     o_all, w_all, h_t, own, pre, snd, half_in, full_in, y_early, acc, gbuf, ubuf, ggbuf, gubuf,
-    o_send, o_recv, w_send, w_recv, wc_send, wc_recv, t_send, t_recv, z_send, z_recv, y_send, y_recv,
+    o_send, w_send, t_send, r_send, o_recv, w_recv, wc_recv, t_recv, half_recv, full_recv, y_recv, end_recv,
     o_local, w_local, in_sem, out_sem, last_sem,
 ):
     TB = og.shape[0]
@@ -61,16 +65,16 @@
     ZP, ZM, YP, CP = dev(dz=1), dev(dz=-1), dev(o=1), dev(cc=1)
     HP, XP, XM = dev(h=1), dev(dx=1), dev(dx=-1)
 
-    sends = []
-
     def send(src, dst, ss, rs, to):
         cp = pltpu.make_async_remote_copy(src, dst, ss, rs, device_id=to, device_id_type=MESH)
         cp.start()
-        sends.append(cp)
         return cp
 
-    def arrived(dst, ss, rs):
-        pltpu.make_async_remote_copy(dst, dst, ss, rs, device_id=CP, device_id_type=MESH).wait_recv()
+    def arrived(like, rs):
+        pltpu.make_async_remote_copy(like, like, o_send, rs, device_id=CP, device_id_type=MESH).wait_recv()
+
+    def sent(like, ss):
+        pltpu.make_async_remote_copy(like, like, ss, end_recv, device_id=CP, device_id_type=MESH).wait_send()
 
     barrier = pltpu.get_barrier_semaphore()
     for to in (ZP, ZM, YP, CP, HP, XP, XM):
@@ -104,17 +108,15 @@
 
     w_own = pltpu.make_async_copy(w, w_all.at[:, w_cols(SLOT[0, 0], 0)], w_local)
     w_own.start()
-    o_own = []
     for k, (dz, o) in enumerate(ORDER):
         for cc in range(2):
             d = ((z + dz + 4) % 4) * 4 + ((yl + o) % 2) * 2 + (c + cc) % 2
             cp = pltpu.make_async_copy(
                 og.at[:, pl.ds(pl.multiple_of(d * BLK, BLK), BLK)],
                 o_all.at[o_rows(0, 0), pl.ds((2 * k + cc) * BLK, BLK)],
-                o_local.at[k, cc],
+                o_local.at[0 if k == FIRST else 1],
             )
             cp.start()
-            o_own.append(cp)
     for slot in range(2):
         for cp in tile_in(slot, slot):
             cp.start()
@@ -130,17 +132,21 @@
             rows = pl.ds(SPLIT, FFD - SPLIT)
         return w_all.at[rows, w_cols(SLOT[dz, o], 0)]
 
-    n_w = itertools.count()
+    def w_size(o, part):
+        return HALF if o == 0 else SPLIT // 2 if part < 2 else FFD - SPLIT
+
+    w_group = {part: i for i, group in enumerate(W_GROUPS) for part in group}
+    w_seen = set()
 
     def w_to(src, dz, o, part, to):
-        send(src, w_part(dz, o, part), w_send.at[next(n_w)], w_recv.at[SLOT[dz, o], part], to)
-
-    w_seen = set()
+        send(src, w_part(dz, o, part), w_send, w_recv.at[w_group[dz, o, part]], to)
 
     def w_got(dz, o, part):
-        if (dz, o, part) not in w_seen:
-            w_seen.add((dz, o, part))
-            arrived(w_part(dz, o, part), w_send.at[0], w_recv.at[SLOT[dz, o], part])
+        i = w_group[dz, o, part]
+        if i not in w_seen:
+            w_seen.add(i)
+            rows = sum(w_size(o, part) for _, o, part in W_GROUPS[i])
+            arrived(w_all.at[pl.ds(0, rows), pl.ds(0, BLK)], w_recv.at[i])
 
     def Wz(p):
         w_to(w.at[pl.ds(p * HALF, HALF), :], -1, 0, p, ZP)
@@ -175,49 +181,47 @@
         k = SLOT[dz, o]
         if (dz, o) == (0, 0):
             w_own.wait()
-        send(w_all.at[:, w_cols(k, 0)], w_all.at[:, w_cols(k, 1)], wc_send.at[k], wc_recv.at[k], CP)
+        send(w_all.at[:, w_cols(k, 0)], w_all.at[:, w_cols(k, 1)], w_send, wc_recv, CP)
 
     def WD():
-        for k in range(len(ORDER)):
-            arrived(w_all.at[:, w_cols(k, 1)], wc_send.at[k], wc_recv.at[k])
+        arrived(w_all.at[:, pl.ds(0, len(ORDER) * BLK)], wc_recv)
 
     def o_to(k, h, dx, part, kind, to):
         ref = o_all.at[o_rows(h, dx, part), o_cols(k)]
-        send(ref, ref, o_send.at[k, kind], o_recv.at[k, kind], to)
-
-    def o_got(k, h, dx, part, kind):
-        ref = o_all.at[o_rows(h, dx, part), o_cols(k)]
-        arrived(ref, o_send.at[k, kind], o_recv.at[k, kind])
+        send(ref, ref, o_send, o_recv.at[k, kind], to)
+
+    def o_got(k, rows, kind):
+        arrived(o_all.at[pl.ds(0, rows), o_cols(k)], o_recv.at[k, kind])
+
+    o_ready = set()
 
     def O0(k):
-        o_own[2 * k].wait()
-        o_own[2 * k + 1].wait()
+        i = 0 if k == FIRST else 1
+        if i not in o_ready:
+            o_ready.add(i)
+            mine = o_all.at[o_rows(0, 0), pl.ds(0, (2 if i == 0 else 14) * BLK)]
+            pltpu.make_async_copy(mine, mine, o_local.at[i]).wait()
         o_to(k, 0, 0, None, 0, HP)
         o_to(k, 0, 0, None, 1, XP)
-        o_to(k, 0, 0, None, 2, XM)
+        o_to(k, 0, 0, None, 1, XM)
 
     def O1a(k):
-        o_got(k, 0, -1, None, 1)
+        o_got(k, 2 * TB, 1)
         o_to(k, 0, -1, 0, 3, XP)
-        o_got(k, 0, 1, None, 2)
-        o_to(k, 0, 1, 1, 4, XM)
+        o_to(k, 0, 1, 1, 3, XM)
 
     def O1b(k):
-        o_got(k, 1, 0, None, 0)
-        o_to(k, 1, 0, None, 5, XP)
-        o_to(k, 1, 0, None, 6, XM)
+        o_got(k, TB, 0)
+        o_to(k, 1, 0, None, 2, XP)
+        o_to(k, 1, 0, None, 2, XM)
 
     def O2(k):
-        o_got(k, 1, -1, None, 5)
-        o_to(k, 1, -1, 0, 7, XP)
-        o_got(k, 1, 1, None, 6)
-        o_to(k, 1, 1, 1, 8, XM)
+        o_got(k, 2 * TB, 2)
+        o_to(k, 1, -1, 0, 3, XP)
+        o_to(k, 1, 1, 1, 3, XM)
 
     def O3(k):
-        o_got(k, 0, 2, 0, 3)
-        o_got(k, 0, 2, 1, 4)
-        o_got(k, 1, 2, 0, 7)
-        o_got(k, 1, 2, 1, 8)
+        o_got(k, 2 * TB, 3)
 
     def H(n):
         slot = n % 2
@@ -257,10 +261,9 @@
     def T(k):
         slot = k % 2
         if k >= 2:
-            t_copies[k - 2].wait_send()
-            sends[:] = [cp for cp in sends if cp is not t_copies[k - 2]]
+            t_copies.pop(k - 2).wait_send()
         term(k, 1, snd.at[slot])
-        t_copies[k] = send(snd.at[slot], pre.at[k], t_send.at[k], t_recv.at[k], CP)
+        t_copies[k] = send(snd.at[slot], pre.at[k], t_send.at[slot], t_recv.at[k], CP)
         term(k, 0, own.at[k])
 
     def row_part(o, p):
@@ -269,7 +272,7 @@
         return (p * (SPLIT2 // 2), SPLIT2 // 2) if p < 2 else (SPLIT2, FFD - SPLIT2)
 
     def add(k, at, size, others):
-        step = 64
+        step = 32
         others = [(pre.at[k], 0, FFD), *others]
         cuts = {at, at + size}
         for _, first, many in others:
@@ -291,29 +294,25 @@
     seen = set()
     last_copies = []
 
-    def once(ref, ss, rs, *name):
-        if name not in seen:
-            seen.add(name)
-            arrived(ref, ss, rs)
-
-    def y_part(dz, p):
-        if dz == 0:
-            at, size = row_part(1, p)
-            return y_in.at[pl.ds(at, size), :], p
-        i = (2, 1, -1).index(dz)
-        return y_early.at[i], 3 + i
-
-    def y_got(dz, p):
-        ref, sem = y_part(dz, p)
-        once(ref, y_send.at[sem], y_recv.at[sem], "y", sem)
+    def t_got(k):
+        if k not in seen:
+            seen.add(k)
+            arrived(pre.at[k], t_recv.at[k])
+
+    def like(rows):
+        return pre.at[0, pl.ds(0, rows), :]
 
     def y_to(k, dz, p):
         at, size = row_part(1, p)
-        ref, sem = y_part(dz, p)
-        send(own.at[k, pl.ds(at, size), :], ref, y_send.at[sem], y_recv.at[sem], YP)
+        src = own.at[k, pl.ds(at, size), :]
+        if dz == 0:
+            send(src, y_in.at[pl.ds(at, size), :], r_send, end_recv, YP)
+        else:
+            i = (2, 1, -1).index(dz)
+            send(src, y_early.at[i], r_send, y_recv.at[i], YP)
 
     def PY(k):
-        once(pre.at[k], t_send.at[k], t_recv.at[k], "t", k)
+        t_got(k)
         at, size = row_part(1, 2)
         add(k, at, size, [])
         y_to(k, ORDER[k][0], 2)
@@ -323,48 +322,49 @@
         at, size = row_part(o, p)
         rows = pl.ds(at, size)
         blk = own.at[k, rows, :]
-        once(pre.at[k], t_send.at[k], t_recv.at[k], "t", k)
+        t_got(k)
         others = []
-        if o == 0 and dz and p == 1:
-            y_got(dz, 2)
-            others.append((y_part(dz, 2)[0], SPLIT2, FFD - SPLIT2))
+        if o == 0 and p == 1:
+            i = (2, 1, -1).index(dz)
+            arrived(y_early.at[i], y_recv.at[i])
+            others.append((y_early.at[i], SPLIT2, FFD - SPLIT2))
         if dz == 2:
             add(k, at, size, others)
-            send(blk, half_in.at[o, p, pl.ds(0, size), :], z_send.at[o, p], z_recv.at[o, p], (ZP, ZM)[p])
+            send(blk, half_in.at[o, p, pl.ds(0, size), :], r_send, half_recv.at[o, p], (ZP, ZM)[p])
         elif dz:
             side = 0 if dz == 1 else 1
             if p == side:
                 ref = half_in.at[o, p, pl.ds(0, size), :]
-                arrived(ref, z_send.at[o, p], z_recv.at[o, p])
+                arrived(ref, half_recv.at[o, p])
                 others.append((ref, at, size))
             add(k, at, size, others)
-            sem = 2 + 2 * side + p
-            dst = full_in.at[side, rows, :] if o else (up_in, down_in)[side].at[rows, :]
-            send(blk, dst, z_send.at[o, sem], z_recv.at[o, sem], (ZP, ZM)[side])
+            if o == 1:
+                send(blk, full_in.at[side, rows, :], r_send, full_recv.at[p], (ZP, ZM)[side])
+            else:
+                send(blk, (up_in, down_in)[side].at[rows, :], r_send, end_recv, (ZP, ZM)[side])
         else:
-            for side in range(2):
-                sem = 2 + 2 * side + p
-                arrived(full_in.at[side, rows, :], z_send.at[o, sem], z_recv.at[o, sem])
-                others.append((full_in.at[side], 0, FFD))
-            add(k, at, size, others)
+            arrived(like(2 * size), full_recv.at[p])
+            add(k, at, size, [(full_in.at[side], 0, FFD) for side in range(2)])
             y_to(k, 0, p)
 
     def Z(p):
         k = SLOT[0, 0]
         if p == 0:
-            once(pre.at[k], t_send.at[k], t_recv.at[k], "t", k)
+            t_got(k)
             add(k, 0, FFD, [])
             cp = pltpu.make_async_copy(own.at[k], last, last_sem)
             cp.start()
             last_copies.append(cp)
             return
-        for half in range(2):
-            rows = pl.ds(half * HALF, HALF)
-            for side, ref in enumerate((up_in, down_in)):
-                sem = 2 + 2 * side + half
-                arrived(ref.at[rows, :], z_send.at[0, sem], z_recv.at[0, sem])
-        for part in range(3):
-            y_got(0, part)
+        for cp in tile_out(NT - 2, (NT - 2) % 2) + tile_out(NT - 1, (NT - 1) % 2) + tuple(last_copies):
+            cp.wait()
+        blocks = len(ORDER)
+        sent(o_all.at[pl.ds(0, 7 * TB), :], o_send)
+        sent(w_all.at[:, pl.ds(0, (2 * blocks - 1) * BLK)], w_send)
+        for cp in t_copies.values():
+            cp.wait_send()
+        sent(pre.at[pl.ds(0, blocks - 1)], r_send)
+        arrived(pre.at[pl.ds(0, 3)], end_recv)
 
     def D(n):
         slot = n % 2
@@ -410,12 +410,6 @@
     )
     for name, *at in SCHEDULE:
         tasks[name](*at)
-    for cp in tile_out(NT - 2, (NT - 2) % 2) + tile_out(NT - 1, (NT - 1) % 2):
-        cp.wait()
-    for cp in last_copies:
-        cp.wait()
-    for cp in sends:
-        cp.wait_send()
 
 
 def finish(norm, gg_in, gu_in, last, up_in, down_in, y_in, gg, gu, gd, total, sem):
@@ -466,19 +460,19 @@
             pltpu.VMEM((2, TOK, BLK), BF16),
             pltpu.VMEM((2, TOK, BLK), BF16),
             pltpu.VMEM((2, TOK, BLK), BF16),
-            dma((n, 9)),
-            dma((n, 9)),
-            dma((18,)),
-            dma((n, 3)),
+            dma,
+            dma,
+            dma((2,)),
+            dma,
+            dma((n, 4)),
+            dma((len(W_GROUPS),)),
+            dma,
             dma((n,)),
-            dma((n,)),
-            dma((n,)),
-            dma((n,)),
-            dma((2, 6)),
-            dma((2, 6)),
-            dma((6,)),
-            dma((6,)),
-            dma((n, 2)),
+            dma((2, 2)),
+            dma((2,)),
+            dma((3,)),
+            dma,
+            dma((2,)),
             dma,
             dma((2, 2)),
             dma((2, 2)),

time: 115 us -> 113 us (0.983)
  Pallas kernels: 114 us -> 112 us
    pallas_call x1, Pallas kernels: 111 us -> 108 us  [shards(): pl.pallas_call(kernel, out_shape=[pltpu.VMEM((TOK, FFD), BF16)] * 2 + [pl...]
where the time goes in v4:
time: 113 us
  Pallas kernels  112 us (99%)
    pallas_call x1, Pallas kernels, shards(): pl.pallas_call(kernel, out_shape=[pltpu.VMEM((TOK, FFD), BF16)] * 2 + [pl...  108 us
    pallas_call x1, Pallas kernels, shards(): pl.pallas_call(functools.partial(finish, 1.0 / math.sqrt(TOK * lax.axis_s...  3.37 us

profile of v4, /device:TPU:0, one launch (start us, length us, event | category | flops | bytes accessed | tf_op | source)
XLA Modules:
  0.0 112.5 jit_solution(8446347720384532959)
XLA Ops:
  0.6 108.3 %shard_map.67 = (bf16[1024,1792]{1,0:T(8,128)(2,1)S(1)}, bf16[1024,1792]{1,0:T(8,128)(2,1)S(1)}, bf16[1792,256]{1,0:T(8,128)(2,1)S(1)}, bf16[1792,256]{1,0:T(8,1...) custom-call(bf16[128,4096]{1,0:T(8,128)(2,1)} %og.1, bf16[1024,1792]{1,0:T(8,128)(2,1)} %gp.1, ...), custom_call_target="tpu_custom_call" | custom-call | flops 30064771072 | bytes 41943040 | tf_op jit(solution)/shard_map/pallas_call | solution.py:443
  109.0 3.4 %shard_map.68 = (bf16[1024,1792]{1,0:T(8,128)(2,1)}, bf16[1024,1792]{1,0:T(8,128)(2,1)}, bf16[1792,256]{1,0:T(8,128)(2,1)}) custom-call(bf16[1024,1792]{1,0:T(8,128)(2,1)S(1)} %get-tuple-element.9.gg_in, bf16[1024,1792]{1,0:T(8,128)(2,1)S(1)} %get-tuple-element.10.gu_in, bf16[1792,256]{1,0:T(8,128)(2,1)S(1)} %get-tuple-element.11.last, ...), custom_call_target="tpu_custom_call" | custom-call | tf_op jit(solution)/shard_map/pallas_call | solution.py:486

commit v5 on v4

--- a/solution.py
+++ b/solution.py
@@ -18,7 +18,7 @@
     ((-1, 0, 0), (1, 0, 1)), ((-1, 0, 1),), ((1, 0, 0),), ((2, 0, 0), (2, 0, 1)), ((0, 1, 0),), ((0, 1, 1),), ((0, 1, 2),),
     ((-1, 1, 0), (1, 1, 1)), ((-1, 1, 1), (-1, 1, 2)), ((1, 1, 0), (1, 1, 2)), ((2, 1, 0), (2, 1, 1), (2, 1, 2)),
 )
-SPLIT = 1184
+SPLIT = 1152
 SPLIT2 = 1280
 FIRST = 1
 VMEM_LIMIT = 51 << 20

time: 113 us -> 112 us (level)
  no operation moved by 1% of the time
where the time goes in v5:
time: 112 us
  Pallas kernels  111 us (99%)
    pallas_call x1, Pallas kernels, shards(): pl.pallas_call(kernel, out_shape=[pltpu.VMEM((TOK, FFD), BF16)] * 2 + [pl...  108 us
    pallas_call x1, Pallas kernels, shards(): pl.pallas_call(functools.partial(finish, 1.0 / math.sqrt(TOK * lax.axis_s...  3.37 us

profile of v5, /device:TPU:0, one launch (start us, length us, event | category | flops | bytes accessed | tf_op | source)
XLA Modules:
  0.0 112.0 jit_solution(14028529636889768633)
XLA Ops:
  0.6 107.8 %shard_map.67 = (bf16[1024,1792]{1,0:T(8,128)(2,1)S(1)}, bf16[1024,1792]{1,0:T(8,128)(2,1)S(1)}, bf16[1792,256]{1,0:T(8,128)(2,1)S(1)}, bf16[1792,256]{1,0:T(8,1...) custom-call(bf16[128,4096]{1,0:T(8,128)(2,1)} %og.1, bf16[1024,1792]{1,0:T(8,128)(2,1)} %gp.1, ...), custom_call_target="tpu_custom_call" | custom-call | flops 30064771072 | bytes 41943040 | tf_op jit(solution)/shard_map/pallas_call | solution.py:443
  108.5 3.4 %shard_map.68 = (bf16[1024,1792]{1,0:T(8,128)(2,1)}, bf16[1024,1792]{1,0:T(8,128)(2,1)}, bf16[1792,256]{1,0:T(8,128)(2,1)}) custom-call(bf16[1024,1792]{1,0:T(8,128)(2,1)S(1)} %get-tuple-element.9.gg_in, bf16[1024,1792]{1,0:T(8,128)(2,1)S(1)} %get-tuple-element.10.gu_in, bf16[1792,256]{1,0:T(8,128)(2,1)S(1)} %get-tuple-element.11.last, ...), custom_call_target="tpu_custom_call" | custom-call | tf_op jit(solution)/shard_map/pallas_call | solution.py:486

commit v6 on v5

--- a/solution.py
+++ b/solution.py
@@ -83,15 +83,18 @@
     def tile_in(n, slot):
         cols = pl.ds(pl.multiple_of(n * BLK, BLK), BLK)
         return (
-            pltpu.make_async_copy(gp.at[:, cols], gbuf.at[slot], in_sem.at[slot, 0]),
-            pltpu.make_async_copy(up.at[:, cols], ubuf.at[slot], in_sem.at[slot, 1]),
+            pltpu.make_async_copy(gp.at[:, cols], gbuf.at[slot], in_sem.at[slot]),
+            pltpu.make_async_copy(up.at[:, cols], ubuf.at[slot], in_sem.at[slot]),
         )
+
+    def both(buf, sem):
+        pltpu.make_async_copy(buf, buf, sem).wait()
 
     def tile_out(n, slot):
         cols = pl.ds(pl.multiple_of(n * BLK, BLK), BLK)
         return (
-            pltpu.make_async_copy(ggbuf.at[slot], gg.at[:, cols], out_sem.at[slot, 0]),
-            pltpu.make_async_copy(gubuf.at[slot], gu.at[:, cols], out_sem.at[slot, 1]),
+            pltpu.make_async_copy(ggbuf.at[slot], gg.at[:, cols], out_sem.at[slot]),
+            pltpu.make_async_copy(gubuf.at[slot], gu.at[:, cols], out_sem.at[slot]),
         )
 
     def o_cols(k):
@@ -225,8 +228,7 @@
 
     def H(n):
         slot = n % 2
-        for cp in tile_in(n, slot):
-            cp.wait()
+        both(gbuf, in_sem.at[slot])
 
         def rows(i, _):
             r = pl.ds(pl.multiple_of(i * 128, 128), 128)
@@ -356,7 +358,9 @@
             cp.start()
             last_copies.append(cp)
             return
-        for cp in tile_out(NT - 2, (NT - 2) % 2) + tile_out(NT - 1, (NT - 1) % 2) + tuple(last_copies):
+        for slot in range(2):
+            both(ggbuf, out_sem.at[slot])
+        for cp in last_copies:
             cp.wait()
         blocks = len(ORDER)
         sent(o_all.at[pl.ds(0, 7 * TB), :], o_send)
@@ -380,12 +384,10 @@
             return 0
 
         lax.fori_loop(0, TOK // 512, mm, 0)
-        for cp in tile_in(n, slot):
-            cp.wait()
+        both(gbuf, in_sem.at[slot])
 
         if n >= 2:
-            for cp in tile_out(n - 2, slot):
-                cp.wait()
+            both(ggbuf, out_sem.at[slot])
 
         def rows(i, _):
             r = pl.ds(pl.multiple_of(i * 64, 64), 64)
@@ -474,8 +476,8 @@
             dma,
             dma((2,)),
             dma,
-            dma((2, 2)),
-            dma((2, 2)),
+            dma((2,)),
+            dma((2,)),
             dma,
         ],
         compiler_params=pltpu.CompilerParams(

time: 112 us -> 112 us (level)
  no operation moved by 1% of the time
where the time goes in v6:
time: 112 us
  Pallas kernels  111 us (99%)
    pallas_call x1, Pallas kernels, shards(): pl.pallas_call(kernel, out_shape=[pltpu.VMEM((TOK, FFD), BF16)] * 2 + [pl...  108 us
    pallas_call x1, Pallas kernels, shards(): pl.pallas_call(functools.partial(finish, 1.0 / math.sqrt(TOK * lax.axis_s...  3.37 us

profile of v6, /device:TPU:0, one launch (start us, length us, event | category | flops | bytes accessed | tf_op | source)
XLA Modules:
  0.0 111.9 jit_solution(2033568921599268715)
XLA Ops:
  0.6 107.8 %shard_map.67 = (bf16[1024,1792]{1,0:T(8,128)(2,1)S(1)}, bf16[1024,1792]{1,0:T(8,128)(2,1)S(1)}, bf16[1792,256]{1,0:T(8,128)(2,1)S(1)}, bf16[1792,256]{1,0:T(8,1...) custom-call(bf16[128,4096]{1,0:T(8,128)(2,1)} %og.1, bf16[1024,1792]{1,0:T(8,128)(2,1)} %gp.1, ...), custom_call_target="tpu_custom_call" | custom-call | flops 30064771072 | bytes 41943040 | tf_op jit(solution)/shard_map/pallas_call | solution.py:445
  108.4 3.4 %shard_map.68 = (bf16[1024,1792]{1,0:T(8,128)(2,1)}, bf16[1024,1792]{1,0:T(8,128)(2,1)}, bf16[1792,256]{1,0:T(8,128)(2,1)}) custom-call(bf16[1024,1792]{1,0:T(8,128)(2,1)S(1)} %get-tuple-element.9.gg_in, bf16[1024,1792]{1,0:T(8,128)(2,1)S(1)} %get-tuple-element.10.gu_in, bf16[1792,256]{1,0:T(8,128)(2,1)S(1)} %get-tuple-element.11.last, ...), custom_call_target="tpu_custom_call" | custom-call | tf_op jit(solution)/shard_map/pallas_call | solution.py:488
